TPU v7x, 32 devices: a whole 2x2x4 slice. The times are simulated.
32 devices in a mesh: groups: 2 (over y), vocab: 4 (over z), mp: 2 (over x), sub: 2 (over core).
Axes of the slice: x: 2, y: 2, z: 4, core: 2. Of those that a mesh axis runs over, the one named last changes fastest.
Arguments:
- previous_embedding: bfloat16 [32768, 4096], P('vocab', ('mp', 'sub')), may hold values from -6 to 6
- tile_source: int32 [32, 8], P(('groups', 'vocab')), parts along dimension 0, may hold values from 0 to 255, as said below
- tile_mask: int32 [32, 8, 128, 128], P(('groups', 'vocab')), parts along dimension 0, may hold values from 0 to 1, as said below
- row_order: int32 [4096], P(('groups', 'vocab')), parts along dimension 0, may hold values from 0 to 2047, as said below
- w_in: bfloat16 [4096, 4096], P('vocab', ('mp', 'sub')), may hold values from -0.09375 to 0.09375
- b_in: float32 [4096], P(('mp', 'sub')), may hold values from -3 to 3
- w_out: bfloat16 [4096, 4096], P(('mp', 'sub'), 'vocab'), may hold values from -0.09375 to 0.09375
- grad_out: bfloat16 [4096, 4096], P(('groups', 'vocab'), ('mp', 'sub')), parts along dimension 0, may hold values from -6 to 6
Outputs:
- grad_w_in: float32 [8192, 4096], P(('groups', 'vocab'), ('mp', 'sub')), parts along dimension 0
- grad_w_out: float32 [8192, 4096], P(('groups', 'mp', 'sub'), 'vocab'), parts along dimension 0
- grad_bias: float32 [8192], P(('groups', 'mp', 'sub')), parts along dimension 0
There are 2 independent parts, one for each index of `groups`. A program takes and returns all parts, laid end to end along the dimension named above; an argument that names none is the same for every part. Nothing has to cross between parts.
Inputs may be any that keep to these rules, and one draw needn't show every extreme that they name: `tile_source`: old tile column c belongs to vocab index c // 64. Among the 32 slots of each aligned group of 4 target blocks, at most 16 name tiles of one vocab index, and in every group some vocab index is named exactly 16 times. Repeated tiles may occur. `tile_mask`: in every slot's tile the ones lie in exactly 64 of the 128 columns, each of which holds at least one one. Each number occurs once, and row_order[i] lies in the same aligned group of 512 rows as i.
All inputs are finite; a program needn't handle non-finite values.
Results may differ from a plain program's by a relative error of at most 0.0085.
Values may be sent and summed in bfloat16 or wider, within the bound.
No kernel may reach another device: no remote copies, remote signals or barrier semaphores. Data moves between devices by JAX's collectives and lax.ppermute only.
A program may use at most 192 MiB of HBM per device.

v0:
```python
import jax
import jax.numpy as jnp
from jax import lax
from jax.sharding import PartitionSpec as P

TILE_SIZE = 128


tanh_scale = 0.7978845608028654
cubic_term = 0.044715


def gelu_parts(values):
    inner_arg = tanh_scale * (values + cubic_term * values * values * values)
    tangent = jnp.tanh(inner_arg)
    activation = 0.5 * values * (1.0 + tangent)
    act_slope = 0.5 * (1.0 + tangent) + 0.5 * values * (1.0 - tangent * tangent) * tanh_scale * (
        1.0 + 3.0 * cubic_term * values * values
    )
    return (activation, act_slope)


def local(previous_embedding, tile_source, tile_mask, row_order, w_in, b_in, w_out, grad_out):
    groups = lax.axis_size("vocab")
    blocks, slots_per = tile_source.shape
    tiles_here = previous_embedding.shape[0] // TILE_SIZE
    columns = previous_embedding.shape[1]
    flat_source = tile_source.reshape(-1)
    owner_dev = flat_source // tiles_here
    local_tile = flat_source % tiles_here
    total_slots = flat_source.shape[0]
    capacity = max(2, 2 * total_slots // groups)
    slot_ids = jnp.arange(total_slots)
    earlier = slot_ids[None, :] < slot_ids[:, None]
    same_owner = owner_dev[None, :] == owner_dev[:, None]
    position = jnp.sum(jnp.where(earlier & same_owner, 1, 0), axis=1).astype(jnp.int32)
    owner_hit = owner_dev[:, None] == jnp.arange(groups)[None, :]
    place_hit = position[:, None] == jnp.arange(capacity)[None, :]
    placed = owner_hit[:, :, None] & place_hit[:, None, :]
    slot_index = owner_dev * capacity + position
    mask_values = tile_mask.astype(jnp.bfloat16)
    requests = jnp.sum(jnp.where(placed, local_tile[:, None, None], 0), axis=0)
    tile_lookup = previous_embedding.reshape(tiles_here, TILE_SIZE, columns)
    found_tiles = jnp.take(
        tile_lookup,
        lax.all_to_all(requests, "vocab", split_axis=0, concat_axis=0, tiled=True),
        axis=0,
    )
    arrived = lax.all_to_all(found_tiles, "vocab", split_axis=0, concat_axis=0, tiled=True)
    picked = arrived.reshape(groups * capacity, TILE_SIZE, columns)[slot_index]
    picked = picked.reshape(blocks, slots_per, TILE_SIZE, columns)
    summed = jnp.einsum("bkrc,bkcd->brd", mask_values, picked, preferred_element_type=jnp.float32)
    counts = jnp.sum(tile_mask, axis=(1, 3))
    inverse = 1.0 / jnp.maximum(counts, 1).astype(jnp.float32)
    mixed = (summed * inverse[:, :, None]).astype(jnp.bfloat16).reshape(blocks * TILE_SIZE, columns)
    rows_here = mixed.shape[0]
    ordered = mixed[row_order % rows_here]
    w_in_full = lax.all_gather(w_in, "vocab", axis=0, tiled=True)
    features = lax.all_gather(ordered, ("mp", "sub"), axis=1, tiled=True)
    preact = jnp.dot(features, w_in_full, preferred_element_type=jnp.float32) + b_in
    activation, act_slope = gelu_parts(preact)
    hidden = activation.astype(jnp.bfloat16)
    w_out_full = lax.all_gather(w_out, "vocab", axis=1, tiled=True)
    cotangent = lax.all_gather(grad_out, ("mp", "sub"), axis=1, tiled=True)
    hidden_grad = lax.dot_general(
        cotangent, w_out_full, (((1,), (1,)), ((), ())), preferred_element_type=jnp.float32
    )
    pre_grad = (hidden_grad * act_slope).astype(jnp.bfloat16)
    grad_bias = lax.psum(jnp.sum(pre_grad.astype(jnp.float32), axis=0), "vocab")
    grad_w_in = lax.psum_scatter(
        lax.dot_general(
            features, pre_grad, (((0,), (0,)), ((), ())), preferred_element_type=jnp.float32
        ).astype(jnp.bfloat16),
        "vocab",
        scatter_dimension=0,
        tiled=True,
    ).astype(jnp.float32)
    grad_w_out = (
        lax.psum_scatter(
            lax.dot_general(
                cotangent, hidden, (((0,), (0,)), ((), ())), preferred_element_type=jnp.float32
            ).astype(jnp.bfloat16),
            "vocab",
            scatter_dimension=0,
            tiled=True,
        )
        .astype(jnp.float32)
        .T
    )
    return (grad_w_in, grad_w_out, grad_bias)


def solution(mesh):
    placed = (
        P("vocab", ("mp", "sub")),
        P(("groups", "vocab"), None),
        P(("groups", "vocab"), None, None, None),
        P(("groups", "vocab")),
        P("vocab", ("mp", "sub")),
        P(("mp", "sub")),
        P(("mp", "sub"), "vocab"),
        P(("groups", "vocab"), ("mp", "sub")),
    )
    return jax.shard_map(
        local,
        mesh=mesh,
        in_specs=placed,
        out_specs=(
            P(("groups", "vocab"), ("mp", "sub")),
            P(("groups", "mp", "sub"), "vocab"),
            P(("groups", "mp", "sub")),
        ),
        check_vma=False,
    )
```

profile of v0, /device:TPU:0, one launch (start us, length us, event | category | flops | bytes accessed | tf_op | source)
XLA Modules:
  0.0 1108.9 jit_solution(13974912469971510343)
XLA Ops:
  7.2 0.8 reshape.249
  8.3 11.7 %all_to_all.20 = s32[4,1,16]{2,1,0:T(1,128)S(1)} all-to-all(s32[4,1,16]{2,1,0:T(1,128)S(1)} %bitcast.43), channel_id=1, replica_groups=mesh['groups'=2,'vocab'=4,'mp'=2,'sub'=2] {'vocab'}, dimensions={0} | all-to-all | bytes 512 | tf_op jit(solution)/shard_map/all_to_all | solution.py:46
  20.1 13.2 %gather_fusion = bf16[64,128,1024]{2,1,0:T(8,128)(2,1)} fusion(bf16[64,128,1024]{2,1,0:T(8,128)(2,1)} %bitcast.40, s32[1024]{0:T(1024)S(1)} %pad_clamp_fusion.2), kind=kCustom, calls=%fused_computation | custom fusion | bytes 33554688 | tf_op jit(solution)/shard_map/jit(_take)/gather | solution.py:44
  33.3 14.2 %broadcast_select_fusion = bf16[4,16,128,1024]{3,2,1,0:T(8,128)(2,1)} fusion(bf16[4,16,128,1024]{3,2,1,0:T(8,128)(2,1)} %bitcast.38, pred[4,16]{1,0:T(4,128)(4,1)S(1)} %compare_and_fusion), kind=kLoop, calls=%fused_computation.3 | loop fusion | flops 8388608 | bytes 33554496 | tf_op jit(solution)/shard_map/jit(_take)/select_n | solution.py:44
  47.5 7.1 all-to-all-start.1
  54.7 0.7 all-gather.10.cloned.1.call-update
  55.5 0.7 copy-done
  56.5 494.7 %all-to-all-done.1 = bf16[4,16,128,1024]{3,2,1,0:T(8,128)(2,1)} async-done(((bf16[4,16,128,1024]{3,2,1,0:T(8,128)(2,1)}), bf16[4,16,128,1024]{3,2,1,0:T(8,128)(2,1)}, u32[]{:S(2)}, u32[]{:S(2)}) %all-to-all-start.1) | async-done | bytes 16777248 | tf_op jit(solution)/shard_map/all_to_all | solution.py:49
  551.1 10.8 gather_fusion.1
  561.9 4.6 fusion.7
  566.6 2.8 gather_fusion.2
  569.4 0.7 all-gather.6.cloned.1.call-update
  570.9 32.0 %all-gather.12.cloned.1.call-done = bf16[512,4096]{1,0:T(8,128)(2,1)} async-done(((bf16[512,1024]{1,0:T(8,128)(2,1)}), bf16[512,4096]{1,0:T(8,128)(2,1)}) %all-gather.12.cloned.1.call-update) | async-done | bytes 4194320 | tf_op jit(solution)/shard_map/all_gather | solution.py:59
  603.0 8.1 fusion.21
  611.1 27.9 %all-gather.6.cloned.1.call-done = bf16[512,4096]{1,0:T(8,128)(2,1)} async-done(((bf16[512,1024]{1,0:T(8,128)(2,1)}), bf16[512,4096]{1,0:T(8,128)(2,1)}) %all-gather.6.cloned.1.call-update) | async-done | bytes 4194320 | tf_op jit(solution)/shard_map/all_gather | solution.py:64
  639.1 151.1 %all-gather.8.cloned.1.call-done = bf16[1024,4096]{1,0:T(8,128)(2,1)} async-done(((bf16[1024,1024]{1,0:T(8,128)(2,1)}), bf16[1024,4096]{1,0:T(8,128)(2,1)}) %all-gather.8.cloned.1.call-update) | async-done | bytes 8388624 | tf_op jit(solution)/shard_map/all_gather | solution.py:63
  790.2 10.4 convert_reduce_fusion
  800.6 6.8 convolution_convert_fusion
  807.5 9.2 convert_bitcast_fusion
  816.7 9.5 psum.7
  826.1 124.4 %reduce-scatter.3.cloned.1.call-done = bf16[1024,1024]{1,0:T(8,128)(2,1)} async-done(((bf16[4096,1024]{1,0:T(8,128)(2,1)}), bf16[1024,1024]{1,0:T(8,128)(2,1)}) %reduce-scatter.3.cloned.1.call-update) | async-done | bytes 2097168 | tf_op jit(solution)/shard_map/reduce_scatter | solution.py:70
  950.5 4.1 convert_element_type.44
  954.6 143.3 %reduce-scatter.5.cloned.1.call-done = bf16[1024,1024]{0,1:T(8,128)(2,1)} async-done(((bf16[4096,1024]{0,1:T(8,128)(2,1)}), bf16[1024,1024]{0,1:T(8,128)(2,1)}) %reduce-scatter.5.cloned.1.call-update) | async-done | bytes 2097168 | tf_op jit(solution)/shard_map/reduce_scatter | solution.py:79
  1097.9 4.1 convert_bitcast_fusion.1
  (36 shorter events, 1.8 us)
Async XLA Ops:
  47.5 7.9 copy-start.1
  47.5 503.6 %all-to-all-start.1 = ((bf16[4,16,128,1024]{3,2,1,0:T(8,128)(2,1)}), bf16[4,16,128,1024]{3,2,1,0:T(8,128)(2,1)}, u32[]{:S(2)}, u32[]{:S(2)}) async-start(bf16[4,16,128,1024]{3,2,1,0:T(8,128)(2,1)} %broadcast_select_fusion), calls=%async_computation.1 | async-start | bytes 33554432 | tf_op jit(solution)/shard_map/all_to_all | solution.py:49
  54.6 1.6 copy-start
  54.6 1.8 copy-start.2
  54.6 516.3 %all-gather.10.cloned.1.call-start = ((), (), s32[]{:S(2)}) async-start(), calls=%async_computation.6 | async-start | bytes 10485760 | tf_op jit(solution)/shard_map/all_gather | solution.py:58
  55.4 547.6 %all-gather.12.cloned.1.call-start = ((), (), s32[]{:S(2)}) async-start(), calls=%async_computation.9 | async-start | bytes 5242880 | tf_op jit(solution)/shard_map/all_gather | solution.py:59
  569.4 69.7 %all-gather.6.cloned.1.call-start = ((), (), s32[]{:S(2)}) async-start(), calls=%async_computation.4 | async-start | bytes 5242880 | tf_op jit(solution)/shard_map/all_gather | solution.py:64
  570.1 220.1 %all-gather.8.cloned.1.call-start = ((), (), s32[]{:S(2)}) async-start(), calls=%async_computation.5 | async-start | bytes 10485760 | tf_op jit(solution)/shard_map/all_gather | solution.py:63
  570.7 219.5 %copy-start.4 = (f32[1024]{0:T(1024)S(1)}, f32[1024]{0:T(1024)}, u32[]{:S(2)}) copy-start(f32[1024]{0:T(1024)} %param.13) | copy-start | bytes 12292
  570.7 379.8 %reduce-scatter.3.cloned.1.call-start = ((), (), s32[]{:S(2)}) async-start(), calls=%async_computation.7 | async-start | bytes 10485760 | tf_op jit(solution)/shard_map/reduce_scatter | solution.py:70
  790.2 10.4 copy-start.3
  807.4 290.5 %reduce-scatter.5.cloned.1.call-start = ((), (), s32[]{:S(2)}) async-start(), calls=%async_computation.8 | async-start | bytes 10485760 | tf_op jit(solution)/shard_map/reduce_scatter | solution.py:79
Sparse Core Ops, SparseCore 0:
  57.0 293.1 all-gather.9
  569.5 33.4 all-gather.11
  604.5 34.4 all-gather.5
  640.5 149.6 all-gather.7
  807.6 142.9 reduce-scatter.2
  952.7 145.1 reduce-scatter.4
where the time goes:
time: 1110 us
  waiting for transfers between devices  975 us (88%)
  matrix products  39.2 us (4%)
  local copies, waits for them, and re-layouts  28.5 us (3%)
  other arithmetic  22.9 us (2%)
  blocking collectives  21.1 us (2%)
  between operations  14.3 us (1%)
    all_to_all x1, waiting for transfers between devices, local(): lax.all_to_all(found_tiles, 'vocab', split_axis=0, concat_axis=0, tiled=T...  495 us
    all_gather x1, waiting for transfers between devices, local(): w_out_full = lax.all_gather(w_out, 'vocab', axis=1, tiled=True)  151 us
    reduce_scatter x1, waiting for transfers between devices, local(): lax.psum_scatter(lax.dot_general(cotangent, hidden, (((0,), (0,)), ((), (...  143 us
    reduce_scatter x1, waiting for transfers between devices, local(): lax.psum_scatter(lax.dot_general(features, pre_grad, (((0,), (0,)), ((),...  124 us
    all_gather x1, waiting for transfers between devices, local(): features = lax.all_gather(ordered, ('mp', 'sub'), axis=1, tiled=True)  32 us
    all_gather x1, waiting for transfers between devices, local(): cotangent = lax.all_gather(grad_out, ('mp', 'sub'), axis=1, tiled=True)  27.9 us
  transfers between devices with their start and end apart: 7, of which 6 were waited for; matrix products, arithmetic and copies ran while one was open for 4% of the time, Pallas kernels for 0%

commit v1 on v0

--- a/solution.py
+++ b/solution.py
@@ -1,6 +1,10 @@
+import functools
+
 import jax
 import jax.numpy as jnp
 from jax import lax
+from jax.experimental import pallas as pl
+from jax.experimental.pallas import tpu as pltpu
 from jax.sharding import PartitionSpec as P
 
 TILE_SIZE = 128
@@ -20,7 +24,273 @@
     return (activation, act_slope)
 
 
-def local(previous_embedding, tile_source, tile_mask, row_order, w_in, b_in, w_out, grad_out):
+TO_MIDDLE = [(0, 1), (3, 2)]
+ACROSS = [(1, 2), (2, 1)]
+TO_END = [(1, 0), (2, 3)]
+SWAP = [(0, 1), (1, 0)]
+
+ROW_TILE = 256
+HIDDEN_CHUNK = 256
+VMEM_BYTES = 56 * 1024 * 1024
+
+
+def planes_fit(mesh):
+    return dict(mesh.shape) == dict(groups=2, vocab=4, mp=2, sub=2)
+
+
+def after(value, *others):
+    return lax.optimization_barrier((value, *others))[0]
+
+
+def mix_kernel(group, places, tile_ids, block_ids, *refs):
+    tiles, (own_masks, sibling_masks, out, total) = refs[:places], refs[places:]
+    total[...] = jnp.zeros_like(total)
+    for place in range(places):
+        half = places // 2
+        mask = own_masks[0, place] if place < half else sibling_masks[0, place - half]
+        start = pl.multiple_of(block_ids[group * places + place] * TILE_SIZE, TILE_SIZE)
+        total[pl.ds(start, TILE_SIZE), :] += jnp.dot(mask, tiles[place][0], preferred_element_type=jnp.float32)
+    out[...] = total[...].astype(out.dtype)
+
+
+def mix_group(group, rows, tile_ids, block_ids, tile_lookup, own_masks, sibling_masks):
+    half = own_masks.shape[1]
+    places = 2 * half
+    columns = tile_lookup.shape[2]
+
+    def tile_spec(place):
+        return pl.BlockSpec((1, TILE_SIZE, columns), lambda i, ids, blocks: (ids[group * places + place], 0, 0))
+
+    mask_spec = pl.BlockSpec((1, half, TILE_SIZE, TILE_SIZE), lambda i, ids, blocks: (group, 0, 0, 0))
+    return pl.pallas_call(
+        functools.partial(mix_kernel, group, places),
+        out_shape=jax.ShapeDtypeStruct((rows, columns), jnp.bfloat16),
+        grid_spec=pltpu.PrefetchScalarGridSpec(
+            num_scalar_prefetch=2,
+            grid=(1,),
+            in_specs=[tile_spec(place) for place in range(places)] + [mask_spec] * 2,
+            out_specs=pl.BlockSpec((rows, columns), lambda i, ids, blocks: (0, 0)),
+            scratch_shapes=[pltpu.VMEM((rows, columns), jnp.float32)],
+        ),
+        compiler_params=pltpu.CompilerParams(vmem_limit_bytes=VMEM_BYTES),
+        cost_estimate=pl.CostEstimate(
+            flops=2 * places * TILE_SIZE * TILE_SIZE * columns,
+            bytes_accessed=2 * places * TILE_SIZE * columns + 2 * rows * columns,
+            transcendentals=0,
+        ),
+        name=f"mix_group_{group}",
+    )(tile_ids, block_ids, *([tile_lookup] * places), own_masks, sibling_masks)
+
+
+def chunk_kernel(scalars, features, cotangent, in_own, in_end, in_far, in_far_half, out_own, out_end, out_far, out_far_half,
+                 bias, grad_in, grad_in_end, grad_out, grad_out_end, grad_bias, in_all, out_all, sum_in, sum_out, sum_bias):
+    step = pl.program_id(0)
+    own, part = scalars[0], scalars[1]
+    width = in_own.shape[0]
+
+    @pl.when(step == 0)
+    def _():
+        sum_in[...] = jnp.zeros_like(sum_in)
+        sum_out[...] = jnp.zeros_like(sum_out)
+        sum_bias[...] = jnp.zeros_like(sum_bias)
+        in_all[own] = in_own[...]
+        in_all[own ^ 1] = in_end[...]
+        out_all[own] = out_own[...]
+        out_all[own ^ 1] = out_end[...]
+        in_half, out_half = in_far.shape[1], out_far.shape[1]
+        for piece, where in ((0, 3), (1, 2)):
+            for source_in, source_out, half in ((in_far, out_far, part), (in_far_half, out_far_half, 1 - part)):
+                in_all[own ^ where, pl.ds(pl.multiple_of(half * in_half, in_half), in_half), :] = source_in[piece]
+                out_all[own ^ where, pl.ds(pl.multiple_of(half * out_half, out_half), out_half), :] = source_out[piece]
+
+    preact = bias[...] + jnp.zeros((features.shape[2], in_own.shape[1]), jnp.float32)
+    hidden_grad = jnp.zeros_like(preact)
+    for k in range(features.shape[1]):
+        preact += jnp.dot(features[0, k], in_all[k], preferred_element_type=jnp.float32)
+        hidden_grad += lax.dot_general(
+            cotangent[0, k], out_all[k], (((1,), (1,)), ((), ())), preferred_element_type=jnp.float32
+        )
+    activation, act_slope = gelu_parts(preact)
+    hidden = activation.astype(jnp.bfloat16)
+    pre_grad = (hidden_grad * act_slope).astype(jnp.bfloat16)
+    sum_bias[...] += jnp.sum(pre_grad.astype(jnp.float32), axis=0, keepdims=True)
+    over_rows = (((0,), (0,)), ((), ()))
+    for j in range(2):
+        sum_in[j] += lax.dot_general(pre_grad, features[0, own ^ j], over_rows, preferred_element_type=jnp.float32)
+        sum_out[j] += lax.dot_general(hidden, cotangent[0, own ^ j], over_rows, preferred_element_type=jnp.float32)
+
+    @pl.when(step == pl.num_programs(0) - 1)
+    def _():
+        grad_in[...] = sum_in[0].T
+        grad_in_end[...] = sum_in[1].T.astype(jnp.bfloat16)
+        grad_out[...] = sum_out[0]
+        grad_out_end[...] = sum_out[1].astype(jnp.bfloat16)
+        grad_bias[...] = sum_bias[...]
+
+
+def hidden_chunk(chunk, scalars, features, cotangent, w_in, w_out, moved_in, moved_out, bias):
+    groups, pieces, rows, width = features.shape
+    tiles = rows // ROW_TILE
+    size = HIDDEN_CHUNK
+
+    def whole(array):
+        return pl.BlockSpec(array.shape, lambda t, s: (0,) * array.ndim)
+
+    row_block = (1, pieces, ROW_TILE, width)
+    in_specs = [
+        pl.BlockSpec(row_block, lambda t, s: (t // tiles, 0, t % tiles, 0)),
+        pl.BlockSpec(row_block, lambda t, s: (s[2] ^ (t // tiles), 0, t % tiles, 0)),
+        pl.BlockSpec((width, size), lambda t, s: (0, chunk)),
+        *[whole(array) for array in moved_in],
+        pl.BlockSpec((size, width), lambda t, s: (chunk, 0)),
+        *[whole(array) for array in moved_out],
+        pl.BlockSpec((1, size), lambda t, s: (0, chunk)),
+    ]
+    shapes = [
+        jax.ShapeDtypeStruct((width, size), jnp.float32),
+        jax.ShapeDtypeStruct((width, size), jnp.bfloat16),
+        jax.ShapeDtypeStruct((size, width), jnp.float32),
+        jax.ShapeDtypeStruct((size, width), jnp.bfloat16),
+        jax.ShapeDtypeStruct((1, size), jnp.float32),
+    ]
+    return pl.pallas_call(
+        chunk_kernel,
+        out_shape=shapes,
+        grid_spec=pltpu.PrefetchScalarGridSpec(
+            num_scalar_prefetch=1,
+            grid=(groups * tiles,),
+            in_specs=in_specs,
+            out_specs=[pl.BlockSpec(shape.shape, lambda t, s: (0, 0)) for shape in shapes],
+            scratch_shapes=[
+                pltpu.VMEM((pieces, width, size), jnp.bfloat16),
+                pltpu.VMEM((pieces, size, width), jnp.bfloat16),
+                pltpu.VMEM((2, size, width), jnp.float32),
+                pltpu.VMEM((2, size, width), jnp.float32),
+                pltpu.VMEM((1, size), jnp.float32),
+            ],
+        ),
+        compiler_params=pltpu.CompilerParams(vmem_limit_bytes=VMEM_BYTES),
+        cost_estimate=pl.CostEstimate(
+            flops=2 * 2 * groups * rows * (pieces + 2) * width * size,
+            bytes_accessed=2 * 2 * groups * pieces * rows * width,
+            transcendentals=groups * rows * size,
+        ),
+        name=f"hidden_chunk_{chunk}",
+    )(scalars, features, cotangent, w_in, *moved_in, w_out, *moved_out, bias)
+
+
+def in_plane(piece):
+    across = lax.ppermute(piece, "mp", SWAP)
+    return [piece, lax.ppermute(piece, "sub", SWAP), across, lax.ppermute(across, "sub", SWAP)]
+
+
+def middle_planes(previous_embedding, tile_source, tile_mask, row_order, w_in, b_in, w_out, grad_out):
+    plane, part, core = lax.axis_index("vocab"), lax.axis_index("groups"), lax.axis_index("sub")
+    column = 2 * lax.axis_index("mp") + core
+    planes = lax.axis_size("vocab")
+    blocks, slots_per = tile_source.shape
+    total_slots = blocks * slots_per
+    tiles_here = previous_embedding.shape[0] // TILE_SIZE
+    columns = previous_embedding.shape[1]
+    tile_lookup = previous_embedding.reshape(tiles_here, TILE_SIZE, columns)
+    rows = row_order.shape[0]
+    places = 2 * total_slots // planes
+    half = places // 2
+
+    all_source = lax.all_gather(tile_source.reshape(1, -1), "vocab", axis=0, tiled=True)
+    slot_ids = jnp.arange(total_slots)
+    earlier = slot_ids[None, :] < slot_ids[:, None]
+
+    def owners_and_places(sources):
+        owner = sources // tiles_here
+        same = owner[..., None, :] == owner[..., :, None]
+        return owner, jnp.sum(jnp.where(earlier & same, 1, 0), axis=-1).astype(jnp.int32)
+
+    owner, position = owners_and_places(tile_source.reshape(-1))
+    my_places = core * half + jnp.arange(half)
+    hit = (owner[:, None, None] == jnp.arange(planes)[None, :, None]) & (
+        position[:, None, None] == my_places[None, None, :]
+    )
+    slot_of = jnp.sum(jnp.where(hit, slot_ids[:, None, None], 0), axis=0)
+    filled = jnp.any(hit, axis=0)
+    sent = jnp.take(tile_mask.reshape(total_slots, TILE_SIZE, TILE_SIZE), slot_of.reshape(-1), axis=0)
+    sent = jnp.where(filled.reshape(-1)[:, None, None], sent, 0).astype(jnp.bfloat16)
+    sent = sent.reshape(planes, half, TILE_SIZE, TILE_SIZE)
+    own_masks = lax.all_to_all(sent, "vocab", split_axis=0, concat_axis=0, tiled=True)
+    sibling_masks = lax.ppermute(own_masks, "sub", SWAP)
+
+    all_owner, all_position = owners_and_places(all_source)
+    both_places = jnp.concatenate([my_places, (1 - core) * half + jnp.arange(half)])
+    mine = (all_owner == plane)[:, :, None] & (all_position[:, :, None] == both_places[None, None, :])
+    tile_ids = jnp.sum(jnp.where(mine, (all_source % tiles_here)[:, :, None], 0), axis=1).reshape(-1)
+    block_ids = jnp.sum(jnp.where(mine, (slot_ids // slots_per)[None, :, None], 0), axis=1).reshape(-1)
+
+    counts = jnp.sum(tile_mask, axis=(1, 3)).reshape(1, rows)
+    inverse = 1.0 / jnp.maximum(counts, 1).astype(jnp.float32)
+    all_inverse = lax.all_gather(inverse, "vocab", axis=0, tiled=True)
+
+    placed = (row_order % rows)[None, :] == jnp.arange(rows)[:, None]
+    cotangent = jnp.dot(placed.astype(jnp.bfloat16), grad_out, preferred_element_type=jnp.float32).astype(jnp.bfloat16)
+    cot_end = lax.ppermute(cotangent, "vocab", TO_MIDDLE)
+    cot_far = lax.ppermute(after(cotangent, own_masks), "vocab", ACROSS)
+    cot_far_end = lax.ppermute(after(cot_end, own_masks), "vocab", ACROSS)
+    cotangents = jnp.stack([jnp.stack(in_plane(piece)) for piece in (cotangent, cot_end, cot_far_end, cot_far)])
+
+    features = []
+    arrived, summed = [], []
+    for group in range(planes):
+        partial = mix_group(group, rows, tile_ids, block_ids, tile_lookup, own_masks, sibling_masks)
+        from_end = lax.ppermute(partial, "vocab", TO_MIDDLE)
+        arrived.append(from_end)
+        side = (partial.astype(jnp.float32) + from_end.astype(jnp.float32)).astype(jnp.bfloat16)
+        other = lax.ppermute(side, "vocab", ACROSS)
+        summed.append(other)
+        mixed = (side.astype(jnp.float32) + other.astype(jnp.float32)) * all_inverse[group][:, None]
+        features.append(jnp.stack(in_plane(mixed.astype(jnp.bfloat16))))
+    features = jnp.stack(features)
+
+    hidden_units = w_in.shape[1]
+    chunks = hidden_units // HIDDEN_CHUNK
+    in_half, out_half = w_in.shape[0] // 2, HIDDEN_CHUNK // 2
+    scalars = jnp.stack([plane ^ column, part, plane]).astype(jnp.int32)
+    bias = b_in.reshape(1, -1)
+    is_middle = (plane == 1) | (plane == 2)
+    before_end = [cot_end, arrived[2], arrived[3], None]
+    before_far = [summed[1], summed[2], summed[3], None]
+    grad_w_in, grad_w_out, grad_bias = [], [], []
+    for chunk in range(chunks):
+        in_here = w_in[:, chunk * HIDDEN_CHUNK : (chunk + 1) * HIDDEN_CHUNK]
+        out_here = w_out[chunk * HIDDEN_CHUNK : (chunk + 1) * HIDDEN_CHUNK]
+        gate = before_end[chunk] if chunk < 3 else in_end
+        in_end = lax.ppermute(after(in_here, gate), "vocab", TO_MIDDLE)
+        out_end = lax.ppermute(after(out_here, gate), "vocab", TO_MIDDLE)
+
+        def my_half(array, size):
+            return lax.dynamic_slice_in_dim(array, part * size, size, axis=0)
+
+        in_halves = jnp.stack([my_half(in_here, in_half), my_half(in_end, in_half)])
+        out_halves = jnp.stack([my_half(out_here, out_half), my_half(out_end, out_half)])
+        gate = before_far[chunk] if chunk < 3 else in_far
+        in_far = lax.ppermute(after(in_halves, gate), "vocab", ACROSS)
+        out_far = lax.ppermute(after(out_halves, gate), "vocab", ACROSS)
+        in_far_half = lax.ppermute(in_far, "groups", SWAP)
+        out_far_half = lax.ppermute(out_far, "groups", SWAP)
+        own_in, end_in, own_out, end_out, chunk_bias = hidden_chunk(
+            chunk, scalars, features, cotangents, w_in, w_out,
+            (in_end, in_far, in_far_half), (out_end, out_far, out_far_half), bias,
+        )
+        got_in = lax.ppermute(end_in, "vocab", TO_END)
+        got_out = lax.ppermute(end_out, "vocab", TO_END)
+        grad_w_in.append(jnp.where(is_middle, own_in, got_in.astype(jnp.float32)))
+        grad_w_out.append(jnp.where(is_middle, own_out, got_out.astype(jnp.float32)))
+        grad_bias.append(chunk_bias)
+    grad_bias = jnp.concatenate(grad_bias, axis=1)
+    got_bias = lax.ppermute(grad_bias, "vocab", TO_END)
+    grad_bias = jnp.where(is_middle, grad_bias, got_bias).reshape(-1)
+    return (jnp.concatenate(grad_w_in, axis=1), jnp.concatenate(grad_w_out, axis=0), grad_bias)
+
+
+def gathered(previous_embedding, tile_source, tile_mask, row_order, w_in, b_in, w_out, grad_out):
     groups = lax.axis_size("vocab")
     blocks, slots_per = tile_source.shape
     tiles_here = previous_embedding.shape[0] // TILE_SIZE
@@ -102,7 +372,7 @@
         P(("groups", "vocab"), ("mp", "sub")),
     )
     return jax.shard_map(
-        local,
+        middle_planes if planes_fit(mesh) else gathered,
         mesh=mesh,
         in_specs=placed,
         out_specs=(

time: 1110 us -> 688 us (0.62)
  waiting for transfers between devices: 975 us -> 340 us
  Pallas kernels: 0 us -> 123 us
  starting transfers between devices: 7.53 us -> 90 us
  matrix products: 39.2 us -> 1.7 us
  blocking collectives: 21.1 us -> 53.4 us
  other arithmetic: 22.9 us -> 45.5 us
  between operations: 14.3 us -> 2.68 us
    all_to_all x1, waiting for transfers between devices: 495 us -> 0.01 us  [middle_planes(): lax.all_to_all(sent, 'vocab', split_axis=0, concat_axis=0, tiled=True)]
    ppermute x0 -> x69, waiting for transfers between devices: none -> 340 us  [the longest x1 81.9 us: middle_planes(): got_bias = lax.ppermute(grad_bias, 'vocab', TO_END)]
    reduce_scatter x2 -> x0, waiting for transfers between devices: 268 us -> none  [the longest x1 143 us: local(): lax.psum_scatter(lax.dot_general(cotangent, hidden, (((0,), (0,)), ((), (...]
    all_gather x4 -> x0, waiting for transfers between devices: 211 us -> none  [the longest x1 151 us: local(): w_out_full = lax.all_gather(w_out, 'vocab', axis=1, tiled=True)]
    pallas_call x0 -> x8, Pallas kernels: none -> 123 us  [the longest x4 98.9 us: hidden_chunk(): pl.pallas_call(chunk_kernel, out_shape=shapes, grid_spec=pltpu.PrefetchSc...]
    ppermute x0 -> x69, starting transfers between devices: none -> 83.7 us  [the longest x4 15.7 us: middle_planes(): out_end = lax.ppermute(after(out_here, gate), 'vocab', TO_MIDDLE)]
    all_gather x0 -> x2, blocking collectives: none -> 53.4 us  [the longest x1 28.9 us: middle_planes(): lax.all_gather(tile_source.reshape(1, -1), 'vocab', axis=0, tiled=True)]
    dot_general x5 -> x1, matrix products: 39.2 us -> 1.7 us  [middle_planes(): jnp.dot(placed.astype(jnp.bfloat16), grad_out, preferred_element_type=jnp...]
  transfers between devices with their start and end apart: 7 -> 70, of which waited for: 6 -> 21; matrix products, arithmetic and copies ran while one was open for 4% -> 8% of each run, Pallas kernels for 0% -> 18%
where the time goes in v1:
time: 688 us; the launch traced here: 679 us
  waiting for transfers between devices  340 us (49%)
  Pallas kernels  123 us (18%)
  starting transfers between devices  90 us (13%)
  blocking collectives  53.4 us (8%)
  other arithmetic  45.5 us (7%)
  local copies, waits for them, and re-layouts  22.3 us (3%)
    pallas_call x4, Pallas kernels, hidden_chunk(): pl.pallas_call(chunk_kernel, out_shape=shapes, grid_spec=pltpu.PrefetchSc...  98.9 us
    ppermute x1, waiting for transfers between devices, middle_planes(): got_bias = lax.ppermute(grad_bias, 'vocab', TO_END)  81.9 us
    ppermute x8, waiting for transfers between devices, in_plane(): across = lax.ppermute(piece, 'mp', SWAP)  75.9 us
    ppermute x4, waiting for transfers between devices, middle_planes(): from_end = lax.ppermute(partial, 'vocab', TO_MIDDLE)  52.9 us
    ppermute x4, waiting for transfers between devices, middle_planes(): in_end = lax.ppermute(after(in_here, gate), 'vocab', TO_MIDDLE)  43.2 us
    ppermute x4, waiting for transfers between devices, middle_planes(): got_in = lax.ppermute(end_in, 'vocab', TO_END)  39.3 us
    all_gather x1, blocking collectives, middle_planes(): lax.all_gather(tile_source.reshape(1, -1), 'vocab', axis=0, tiled=True)  28.9 us
    all_gather x1, blocking collectives, middle_planes(): all_inverse = lax.all_gather(inverse, 'vocab', axis=0, tiled=True)  24.5 us
  transfers between devices with their start and end apart: 70, of which 21 were waited for; matrix products, arithmetic and copies ran while one was open for 8% of the time, Pallas kernels for 18%

profile of v1, /device:TPU:0, one launch (start us, length us, event | category | flops | bytes accessed | tf_op | source)
XLA Modules:
  0.0 678.9 jit_solution(17371724030785788221)
XLA Ops:
  28.7 28.9 %all-gather = s32[4,1,32]{2,1,0:T(1,128)S(1)} all-gather(s32[1,1,32]{2,1,0:T(1,128)S(1)} %reshape.293), channel_id=1, replica_groups=mesh['groups'=2,'vocab'=4,'mp'=2,'sub'=2] {'vocab'}, dimensions={0}, use_global_device_ids=true | all-gather | bytes 640 | tf_op jit(solution)/shard_map/all_gather | solution.py:200
  68.9 11.3 %collective-permute-done.36.in_end = bf16[1024,256]{1,0:T(8,128)(2,1)S(1)} collective-permute-done((bf16[1024,256]{1,0:T(8,128)(2,1)}, bf16[1024,256]{1,0:T(8,128)(2,1)S(1)}, u32[]{:S(2)}, u32[]{:S(2)}) %collective-permute-start.36) | collective-permute-done | bytes 524320 | tf_op jit(solution)/shard_map/ppermute | solution.py:265
  89.5 24.5 %all-gather.1 = f32[4,1,512]{2,1,0:T(1,128)S(1)} all-gather(f32[1,1,512]{2,1,0:T(1,128)S(1)} %bitcast.187), channel_id=1, replica_groups=mesh['groups'=2,'vocab'=4,'mp'=2,'sub'=2] {'vocab'}, dimensions={0}, use_global_device_ids=true | all-gather | bytes 10240 | tf_op jit(solution)/shard_map/all_gather | solution.py:230
  162.9 52.9 %collective-permute-done.16 = bf16[512,1024]{1,0:T(8,128)(2,1)S(1)} collective-permute-done((bf16[512,1024]{1,0:T(8,128)(2,1)}, bf16[512,1024]{1,0:T(8,128)(2,1)S(1)}, u32[]{:S(2)}, u32[]{:S(2)}) %collective-permute-start.16) | collective-permute-done | bytes 1048608 | tf_op jit(solution)/shard_map/ppermute | solution.py:243
  224.3 26.0 %collective-permute-done.50.in_end = bf16[1024,256]{1,0:T(8,128)(2,1)S(1)} collective-permute-done((bf16[1024,256]{1,0:T(8,128)(2,1)S(1)}, bf16[1024,256]{1,0:T(8,128)(2,1)S(1)}, u32[]{:S(2)}, u32[]{:S(2)}) %collective-permute-start.50) | collective-permute-done | bytes 524320 | tf_op jit(solution)/shard_map/ppermute | solution.py:265
  258.5 8.4 %collective-permute-done.53.out_end = bf16[256,1024]{1,0:T(8,128)(2,1)S(1)} collective-permute-done((bf16[256,1024]{1,0:T(8,128)(2,1)S(1)}, bf16[256,1024]{1,0:T(8,128)(2,1)S(1)}, u32[]{:S(2)}, u32[]{:S(2)}) %collective-permute-start.53) | collective-permute-done | bytes 524320 | tf_op jit(solution)/shard_map/ppermute | solution.py:266
  278.3 6.4 collective-permute-done.60.out_end
  296.3 17.4 %collective-permute-done.4 = bf16[512,1024]{1,0:T(8,128)(2,1)S(1)} collective-permute-done((bf16[512,1024]{1,0:T(8,128)(2,1)S(1)}, bf16[512,1024]{1,0:T(8,128)(2,1)S(1)}, u32[]{:S(2)}, u32[]{:S(2)}) %collective-permute-start.4) | collective-permute-done | bytes 1048608 | tf_op jit(solution)/shard_map/ppermute | solution.py:183
  314.2 21.9 %collective-permute-done.9 = bf16[512,1024]{1,0:T(8,128)(2,1)S(1)} collective-permute-done((bf16[512,1024]{1,0:T(8,128)(2,1)S(1)}, bf16[512,1024]{1,0:T(8,128)(2,1)S(1)}, u32[]{:S(2)}, u32[]{:S(2)}) %collective-permute-start.9) | collective-permute-done | bytes 1048608 | tf_op jit(solution)/shard_map/ppermute | solution.py:183
  336.7 22.0 %collective-permute-done.14 = bf16[512,1024]{1,0:T(8,128)(2,1)S(1)} collective-permute-done((bf16[512,1024]{1,0:T(8,128)(2,1)S(1)}, bf16[512,1024]{1,0:T(8,128)(2,1)S(1)}, u32[]{:S(2)}, u32[]{:S(2)}) %collective-permute-start.14) | collective-permute-done | bytes 1048608 | tf_op jit(solution)/shard_map/ppermute | solution.py:183
  358.6 6.9 %pad_maximum_fusion.1.cotangent = bf16[4,4,512,1024]{3,2,1,0:T(8,128)(2,1)} fusion(bf16[1,4,512,1024]{3,2,1,0:T(8,128)(2,1)S(1)} %maximum_bitcast_fusion.7, bf16[1,4,512,1024]{3,2,1,0:T(8,128)(2,1)S(1)} %maximum_bitcast_fusion.6, bf16[1,4,512,1024]{3,2,1,0:T(8,128)(2,1)S(1)} %maximum_bitcast_fusion.5, bf16[1,4,512,1024]{3,2,1,0:T(8,128)(2,1)S(1)} %maximum_bitcast_fusion.4), kind=kLoop, calls=%fused_computation.2 | loop fusion | flops 25165824 | bytes 33554432 | tf_op jit(solution)/shard_map/stack | solution.py:237
  365.6 14.7 %collective-permute-done.19 = bf16[512,1024]{1,0:T(8,128)(2,1)S(1)} collective-permute-done((bf16[512,1024]{1,0:T(8,128)(2,1)S(1)}, bf16[512,1024]{1,0:T(8,128)(2,1)S(1)}, u32[]{:S(2)}, u32[]{:S(2)}) %collective-permute-start.19) | collective-permute-done | bytes 1048608 | tf_op jit(solution)/shard_map/ppermute | solution.py:183
  389.2 6.9 %pad_maximum_fusion.features = bf16[4,4,512,1024]{3,2,1,0:T(8,128)(2,1)} fusion(bf16[1,4,512,1024]{3,2,1,0:T(8,128)(2,1)S(1)} %maximum_bitcast_fusion.3, bf16[1,4,512,1024]{3,2,1,0:T(8,128)(2,1)S(1)} %maximum_bitcast_fusion.2, bf16[1,4,512,1024]{3,2,1,0:T(8,128)(2,1)S(1)} %maximum_bitcast_fusion.1, bf16[1,4,512,1024]{3,2,1,0:T(8,128)(2,1)S(1)} %maximum_bitcast_fusion), kind=kLoop, calls=%fused_computation.1 | loop fusion | flops 25165824 | bytes 33554432 | tf_op jit(solution)/shard_map/stack | solution.py:250
  402.5 10.1 %collective-permute-done.41.out_far_half = bf16[2,128,1024]{2,1,0:T(8,128)(2,1)S(1)} collective-permute-done((bf16[2,128,1024]{2,1,0:T(8,128)(2,1)S(1)}, bf16[2,128,1024]{2,1,0:T(8,128)(2,1)S(1)}, u32[]{:S(2)}, u32[]{:S(2)}) %collective-permute-start.41) | collective-permute-done | bytes 524320 | tf_op jit(solution)/shard_map/ppermute | solution.py:277
  413.8 24.8 %hidden_chunk_0.1 = (f32[1024,256]{1,0:T(8,128)}, bf16[1024,256]{1,0:T(8,128)(2,1)}, f32[256,1024]{1,0:T(8,128)}, bf16[256,1024]{1,0:T(8,128)(2,1)}, f32[1,256]{1,0:T(1,128)}) custom-call(s32[3]{0:T(128)} %pad_add_fusion.scalars, bf16[4,4,512,1024]{3,2,1,0:T(8,128)(2,1)} %pad_maximum_fusion.features, bf16[4,4,512,1024]{3,2,1,0:T(8,128)(2,1)} %pad_maximum_fusion.1.cotangent, ...), custom_call_target="tpu_custom_call" | custom-call | flops 12884901888 | bytes 33554432 | tf_op jit(solution)/shard_map/hidden_chunk_0/pallas_call | solution.py:156
  444.0 24.7 %hidden_chunk_1.1 = (f32[1024,256]{1,0:T(8,128)}, bf16[1024,256]{1,0:T(8,128)(2,1)}, f32[256,1024]{1,0:T(8,128)}, bf16[256,1024]{1,0:T(8,128)(2,1)}, f32[1,256]{1,0:T(1,128)}) custom-call(s32[3]{0:T(128)} %pad_add_fusion.scalars, bf16[4,4,512,1024]{3,2,1,0:T(8,128)(2,1)} %pad_maximum_fusion.features, bf16[4,4,512,1024]{3,2,1,0:T(8,128)(2,1)} %pad_maximum_fusion.1.cotangent, ...), custom_call_target="tpu_custom_call" | custom-call | flops 12884901888 | bytes 33554432 | tf_op jit(solution)/shard_map/hidden_chunk_1/pallas_call | solution.py:156
  471.3 24.7 %hidden_chunk_2.1 = (f32[1024,256]{1,0:T(8,128)}, bf16[1024,256]{1,0:T(8,128)(2,1)}, f32[256,1024]{1,0:T(8,128)}, bf16[256,1024]{1,0:T(8,128)(2,1)}, f32[1,256]{1,0:T(1,128)}) custom-call(s32[3]{0:T(128)} %pad_add_fusion.scalars, bf16[4,4,512,1024]{3,2,1,0:T(8,128)(2,1)} %pad_maximum_fusion.features, bf16[4,4,512,1024]{3,2,1,0:T(8,128)(2,1)} %pad_maximum_fusion.1.cotangent, ...), custom_call_target="tpu_custom_call" | custom-call | flops 12884901888 | bytes 33554432 | tf_op jit(solution)/shard_map/hidden_chunk_2/pallas_call | solution.py:156
  497.7 24.7 %hidden_chunk_3.1 = (f32[1024,256]{1,0:T(8,128)}, bf16[1024,256]{1,0:T(8,128)(2,1)}, f32[256,1024]{1,0:T(8,128)}, bf16[256,1024]{1,0:T(8,128)(2,1)}, f32[1,256]{1,0:T(1,128)}) custom-call(s32[3]{0:T(128)} %pad_add_fusion.scalars, bf16[4,4,512,1024]{3,2,1,0:T(8,128)(2,1)} %pad_maximum_fusion.features, bf16[4,4,512,1024]{3,2,1,0:T(8,128)(2,1)} %pad_maximum_fusion.1.cotangent, ...), custom_call_target="tpu_custom_call" | custom-call | flops 12884901888 | bytes 33554432 | tf_op jit(solution)/shard_map/hidden_chunk_3/pallas_call | solution.py:156
  527.2 81.9 %collective-permute-done.68 = f32[1,1024]{1,0:T(1,128)S(1)} collective-permute-done((f32[1,1024]{1,0:T(1,128)S(1)}, f32[1,1024]{1,0:T(1,128)S(1)}, u32[]{:S(2)}, u32[]{:S(2)}) %collective-permute-start.68) | collective-permute-done | bytes 4128 | tf_op jit(solution)/shard_map/ppermute | solution.py:288
  623.5 9.7 %collective-permute-done.67 = bf16[256,1024]{1,0:T(8,128)(2,1)S(1)} collective-permute-done((bf16[256,1024]{1,0:T(8,128)(2,1)}, bf16[256,1024]{1,0:T(8,128)(2,1)S(1)}, u32[]{:S(2)}, u32[]{:S(2)}) %collective-permute-start.67) | collective-permute-done | bytes 524320 | tf_op jit(solution)/shard_map/ppermute | solution.py:283
  633.5 11.0 %collective-permute-done.42 = bf16[1024,256]{1,0:T(8,128)(2,1)S(1)} collective-permute-done((bf16[1024,256]{1,0:T(8,128)(2,1)}, bf16[1024,256]{1,0:T(8,128)(2,1)S(1)}, u32[]{:S(2)}, u32[]{:S(2)}) %collective-permute-start.42) | collective-permute-done | bytes 524320 | tf_op jit(solution)/shard_map/ppermute | solution.py:282
  644.6 11.1 %collective-permute-done.49 = bf16[1024,256]{1,0:T(8,128)(2,1)S(1)} collective-permute-done((bf16[1024,256]{1,0:T(8,128)(2,1)}, bf16[1024,256]{1,0:T(8,128)(2,1)S(1)}, u32[]{:S(2)}, u32[]{:S(2)}) %collective-permute-start.49) | collective-permute-done | bytes 524320 | tf_op jit(solution)/shard_map/ppermute | solution.py:282
  658.5 8.5 %collective-permute-done.56 = bf16[1024,256]{1,0:T(8,128)(2,1)S(1)} collective-permute-done((bf16[1024,256]{1,0:T(8,128)(2,1)}, bf16[1024,256]{1,0:T(8,128)(2,1)S(1)}, u32[]{:S(2)}, u32[]{:S(2)}) %collective-permute-start.56) | collective-permute-done | bytes 524320 | tf_op jit(solution)/shard_map/ppermute | solution.py:282
  667.1 8.6 %collective-permute-done.63 = bf16[1024,256]{1,0:T(8,128)(2,1)S(1)} collective-permute-done((bf16[1024,256]{1,0:T(8,128)(2,1)S(1)}, bf16[1024,256]{1,0:T(8,128)(2,1)S(1)}, u32[]{:S(2)}, u32[]{:S(2)}) %collective-permute-start.63) | collective-permute-done | bytes 524320 | tf_op jit(solution)/shard_map/ppermute | solution.py:282
  (354 shorter events, 188.1 us)
Async XLA Ops:
  5.9 53.2 %all-to-all-start = ((bf16[4,8,128,128]{3,2,1,0:T(8,128)(2,1)}), bf16[4,8,128,128]{3,2,1,0:T(8,128)(2,1)S(1)}, u32[]{:S(2)}, u32[]{:S(2)}) async-start(bf16[4,8,128,128]{3,2,1,0:T(8,128)(2,1)} %select_convert_fusion), calls=%async_computation | async-start | bytes 2097152 | tf_op jit(solution)/shard_map/all_to_all | solution.py:219
  18.9 49.3 %collective-permute-start.22 = (bf16[512,1024]{1,0:T(8,128)(2,1)}, bf16[512,1024]{1,0:T(8,128)(2,1)}, u32[]{:S(2)}, u32[]{:S(2)}) collective-permute-start(bf16[512,1024]{1,0:T(8,128)(2,1)} %convolution_convert_fusion), channel_id=1, source_target_pairs={{0,2},{2,0},{1,3},{3,1},{4,6},{6,4},{5,7},{7,5},{8,10},{10,8},{9,1... | collective-permute-start | bytes 3145736 | tf_op jit(solution)/shard_map/ppermute | solution.py:183
  68.2 56.4 %collective-permute-start.25 = (bf16[512,1024]{1,0:T(8,128)(2,1)}, bf16[512,1024]{1,0:T(8,128)(2,1)}, u32[]{:S(2)}, u32[]{:S(2)}) collective-permute-start(bf16[512,1024]{1,0:T(8,128)(2,1)} %collective-permute-done.24), channel_id=1, source_target_pairs={{0,1},{1,0},{2,3},{3,2},{4,5},{5,4},{6,7},{7,6},{8,9},{9,8},{10,11... | collective-permute-start | bytes 3145736 | tf_op jit(solution)/shard_map/ppermute | solution.py:184
  68.5 81.3 %collective-permute-start.23 = (bf16[512,1024]{1,0:T(8,128)(2,1)}, bf16[512,1024]{1,0:T(8,128)(2,1)}, u32[]{:S(2)}, u32[]{:S(2)}) collective-permute-start(bf16[512,1024]{1,0:T(8,128)(2,1)} %collective-permute-done.22), channel_id=1, source_target_pairs={{0,1},{1,0},{2,3},{3,2},{4,5},{5,4},{6,7},{7,6},{8,9},{9,8},{10,11... | collective-permute-start | bytes 3145736 | tf_op jit(solution)/shard_map/ppermute | solution.py:184
  80.2 70.9 %collective-permute-start.28 = (bf16[512,1024]{1,0:T(8,128)(2,1)}, bf16[512,1024]{1,0:T(8,128)(2,1)}, u32[]{:S(2)}, u32[]{:S(2)}) collective-permute-start(bf16[512,1024]{1,0:T(8,128)(2,1)} %collective-permute-done.24), channel_id=1, source_target_pairs={{4,8},{8,4},{5,9},{9,5},{6,10},{10,6},{7,11},{11,7},{20,24},{24,20... | collective-permute-start | bytes 3145736 | tf_op jit(solution)/shard_map/ppermute | solution.py:236
  81.9 70.7 %collective-permute-start.27 = (bf16[512,1024]{1,0:T(8,128)(2,1)}, bf16[512,1024]{1,0:T(8,128)(2,1)}, u32[]{:S(2)}, u32[]{:S(2)}) collective-permute-start(bf16[512,1024]{1,0:T(8,128)(2,1)} %collective-permute-done.26), channel_id=1, source_target_pairs={{0,1},{1,0},{2,3},{3,2},{4,5},{5,4},{6,7},{7,6},{8,9},{9,8},{10,11... | collective-permute-start | bytes 3145736 | tf_op jit(solution)/shard_map/ppermute | solution.py:184
  149.8 70.8 %collective-permute-start.1 = (bf16[512,1024]{1,0:T(8,128)(2,1)S(1)}, bf16[512,1024]{1,0:T(8,128)(2,1)S(1)}, u32[]{:S(2)}, u32[]{:S(2)}) collective-permute-start(bf16[512,1024]{1,0:T(8,128)(2,1)S(1)} %copy-done.5), channel_id=1, source_target_pairs={{0,4},{12,8},{1,5},{13,9},{2,6},{14,10},{3,7},{15,11},{16,20},{28,... | collective-permute-start | bytes 3145736 | tf_op jit(solution)/shard_map/ppermute | solution.py:243
  151.1 70.9 %collective-permute-start.6 = (bf16[512,1024]{1,0:T(8,128)(2,1)S(1)}, bf16[512,1024]{1,0:T(8,128)(2,1)S(1)}, u32[]{:S(2)}, u32[]{:S(2)}) collective-permute-start(bf16[512,1024]{1,0:T(8,128)(2,1)S(1)} %copy-done.4), channel_id=1, source_target_pairs={{0,4},{12,8},{1,5},{13,9},{2,6},{14,10},{3,7},{15,11},{16,20},{28,... | collective-permute-start | bytes 3145736 | tf_op jit(solution)/shard_map/ppermute | solution.py:243
  152.5 63.3 %collective-permute-start.16 = (bf16[512,1024]{1,0:T(8,128)(2,1)}, bf16[512,1024]{1,0:T(8,128)(2,1)S(1)}, u32[]{:S(2)}, u32[]{:S(2)}) collective-permute-start(bf16[512,1024]{1,0:T(8,128)(2,1)} %mix_group_3.1), channel_id=1, source_target_pairs={{0,4},{12,8},{1,5},{13,9},{2,6},{14,10},{3,7},{15,11},{16,20},{28,... | collective-permute-start | bytes 3145736 | tf_op jit(solution)/shard_map/ppermute | solution.py:243
  159.1 95.5 %collective-permute-start.30 = (bf16[512,1024]{1,0:T(8,128)(2,1)}, bf16[512,1024]{1,0:T(8,128)(2,1)S(1)}, u32[]{:S(2)}, u32[]{:S(2)}) collective-permute-start(bf16[512,1024]{1,0:T(8,128)(2,1)} %collective-permute-done.28), channel_id=1, source_target_pairs={{0,2},{2,0},{1,3},{3,1},{4,6},{6,4},{5,7},{7,5},{8,10},{10,8},{9,1... | collective-permute-start | bytes 3145736 | tf_op jit(solution)/shard_map/ppermute | solution.py:183
  159.7 96.3 %collective-permute-start.34 = (bf16[512,1024]{1,0:T(8,128)(2,1)}, bf16[512,1024]{1,0:T(8,128)(2,1)S(1)}, u32[]{:S(2)}, u32[]{:S(2)}) collective-permute-start(bf16[512,1024]{1,0:T(8,128)(2,1)} %collective-permute-done.32), channel_id=1, source_target_pairs={{0,2},{2,0},{1,3},{3,1},{4,6},{6,4},{5,7},{7,5},{8,10},{10,8},{9,1... | collective-permute-start | bytes 3145736 | tf_op jit(solution)/shard_map/ppermute | solution.py:183
  292.0 66.7 %collective-permute-start.14 = (bf16[512,1024]{1,0:T(8,128)(2,1)S(1)}, bf16[512,1024]{1,0:T(8,128)(2,1)S(1)}, u32[]{:S(2)}, u32[]{:S(2)}) collective-permute-start(bf16[512,1024]{1,0:T(8,128)(2,1)S(1)} %multiply_convert_fusion.1), channel_id=1, source_target_pairs={{0,2},{2,0},{1,3},{3,1},{4,6},{6,4},{5,7},{7,5},{8,10},{10,8},{9,1... | collective-permute-start | bytes 3145736 | tf_op jit(solution)/shard_map/ppermute | solution.py:183
  313.7 67.6 %collective-permute-start.13 = (bf16[512,1024]{1,0:T(8,128)(2,1)S(1)}, bf16[512,1024]{1,0:T(8,128)(2,1)S(1)}, u32[]{:S(2)}, u32[]{:S(2)}) collective-permute-start(bf16[512,1024]{1,0:T(8,128)(2,1)S(1)} %multiply_convert_fusion.1), channel_id=1, source_target_pairs={{0,1},{1,0},{2,3},{3,2},{4,5},{5,4},{6,7},{7,6},{8,9},{9,8},{10,11... | collective-permute-start | bytes 3145736 | tf_op jit(solution)/shard_map/ppermute | solution.py:184
  313.7 66.5 %collective-permute-start.19 = (bf16[512,1024]{1,0:T(8,128)(2,1)S(1)}, bf16[512,1024]{1,0:T(8,128)(2,1)S(1)}, u32[]{:S(2)}, u32[]{:S(2)}) collective-permute-start(bf16[512,1024]{1,0:T(8,128)(2,1)S(1)} %multiply_convert_fusion), channel_id=1, source_target_pairs={{0,2},{2,0},{1,3},{3,1},{4,6},{6,4},{5,7},{7,5},{8,10},{10,8},{9,1... | collective-permute-start | bytes 3145736 | tf_op jit(solution)/shard_map/ppermute | solution.py:183
  385.8 52.7 %collective-permute-start.54 = (bf16[2,128,1024]{2,1,0:T(8,128)(2,1)S(1)}, bf16[2,128,1024]{2,1,0:T(8,128)(2,1)S(1)}, u32[]{:S(2)}, u32[]{:S(2)}) collective-permute-start(bf16[2,128,1024]{2,1,0:T(8,128)(2,1)S(1)} %pad_maximum_fusion.9), channel_id=1, source_target_pairs={{4,8},{8,4},{5,9},{9,5},{6,10},{10,6},{7,11},{11,7},{20,24},{24,20... | collective-permute-start | bytes 1572872 | tf_op jit(solution)/shard_map/ppermute | solution.py:275
  440.7 55.4 %collective-permute-start.59 = (bf16[2,512,256]{2,1,0:T(8,128)(2,1)S(1)}, bf16[2,512,256]{2,1,0:T(8,128)(2,1)S(1)}, u32[]{:S(2)}, u32[]{:S(2)}) collective-permute-start(bf16[2,512,256]{2,1,0:T(8,128)(2,1)S(1)} %collective-permute-done.58.in_far), channel_id=1, source_target_pairs={{0,16},{16,0},{1,17},{17,1},{2,18},{18,2},{3,19},{19,3},{4,20},{20... | collective-permute-start | bytes 1572872 | tf_op jit(solution)/shard_map/ppermute | solution.py:276
  441.6 54.5 %collective-permute-start.62 = (bf16[2,128,1024]{2,1,0:T(8,128)(2,1)S(1)}, bf16[2,128,1024]{2,1,0:T(8,128)(2,1)S(1)}, u32[]{:S(2)}, u32[]{:S(2)}) collective-permute-start(bf16[2,128,1024]{2,1,0:T(8,128)(2,1)S(1)} %collective-permute-done.61.out_far), channel_id=1, source_target_pairs={{0,16},{16,0},{1,17},{17,1},{2,18},{18,2},{3,19},{19,3},{4,20},{20... | collective-permute-start | bytes 1572872 | tf_op jit(solution)/shard_map/ppermute | solution.py:277
  442.7 168.3 %collective-permute-start.64 = (bf16[256,1024]{1,0:T(8,128)(2,1)}, bf16[256,1024]{1,0:T(8,128)(2,1)S(1)}, u32[]{:S(2)}, u32[]{:S(2)}) collective-permute-start(bf16[256,1024]{1,0:T(8,128)(2,1)} %get-tuple-element.68), channel_id=1, source_target_pairs={{4,0},{8,12},{5,1},{9,13},{6,2},{10,14},{7,3},{11,15},{20,16},{24,... | collective-permute-start | bytes 1572872 | tf_op jit(solution)/shard_map/ppermute | solution.py:283
  468.8 144.7 %collective-permute-start.65 = (bf16[256,1024]{1,0:T(8,128)(2,1)}, bf16[256,1024]{1,0:T(8,128)(2,1)}, u32[]{:S(2)}, u32[]{:S(2)}) collective-permute-start(bf16[256,1024]{1,0:T(8,128)(2,1)} %get-tuple-element.70), channel_id=1, source_target_pairs={{4,0},{8,12},{5,1},{9,13},{6,2},{10,14},{7,3},{11,15},{20,16},{24,... | collective-permute-start | bytes 1572872 | tf_op jit(solution)/shard_map/ppermute | solution.py:283
  523.2 85.9 %collective-permute-start.68 = (f32[1,1024]{1,0:T(1,128)S(1)}, f32[1,1024]{1,0:T(1,128)S(1)}, u32[]{:S(2)}, u32[]{:S(2)}) collective-permute-start(f32[1,1024]{1,0:T(1,128)S(1)} %constant_dynamic-update-slice_fusion), channel_id=1, source_target_pairs={{4,0},{8,12},{5,1},{9,13},{6,2},{10,14},{7,3},{11,15},{20,16},{24,... | collective-permute-start | bytes 12296 | tf_op jit(solution)/shard_map/ppermute | solution.py:288
  524.5 97.5 %collective-permute-start.66 = (bf16[256,1024]{1,0:T(8,128)(2,1)}, bf16[256,1024]{1,0:T(8,128)(2,1)S(1)}, u32[]{:S(2)}, u32[]{:S(2)}) collective-permute-start(bf16[256,1024]{1,0:T(8,128)(2,1)} %get-tuple-element.72), channel_id=1, source_target_pairs={{4,0},{8,12},{5,1},{9,13},{6,2},{10,14},{7,3},{11,15},{20,16},{24,... | collective-permute-start | bytes 1572872 | tf_op jit(solution)/shard_map/ppermute | solution.py:283
  525.9 107.3 %collective-permute-start.67 = (bf16[256,1024]{1,0:T(8,128)(2,1)}, bf16[256,1024]{1,0:T(8,128)(2,1)S(1)}, u32[]{:S(2)}, u32[]{:S(2)}) collective-permute-start(bf16[256,1024]{1,0:T(8,128)(2,1)} %get-tuple-element.74), channel_id=1, source_target_pairs={{4,0},{8,12},{5,1},{9,13},{6,2},{10,14},{7,3},{11,15},{20,16},{24,... | collective-permute-start | bytes 1572872 | tf_op jit(solution)/shard_map/ppermute | solution.py:283
  613.5 53.5 %collective-permute-start.56 = (bf16[1024,256]{1,0:T(8,128)(2,1)}, bf16[1024,256]{1,0:T(8,128)(2,1)S(1)}, u32[]{:S(2)}, u32[]{:S(2)}) collective-permute-start(bf16[1024,256]{1,0:T(8,128)(2,1)} %get-tuple-element.60), channel_id=1, source_target_pairs={{4,0},{8,12},{5,1},{9,13},{6,2},{10,14},{7,3},{11,15},{20,16},{24,... | collective-permute-start | bytes 1572872 | tf_op jit(solution)/shard_map/ppermute | solution.py:282
  622.0 53.7 %collective-permute-start.63 = (bf16[1024,256]{1,0:T(8,128)(2,1)S(1)}, bf16[1024,256]{1,0:T(8,128)(2,1)S(1)}, u32[]{:S(2)}, u32[]{:S(2)}) collective-permute-start(bf16[1024,256]{1,0:T(8,128)(2,1)S(1)} %copy-done.58), channel_id=1, source_target_pairs={{4,0},{8,12},{5,1},{9,13},{6,2},{10,14},{7,3},{11,15},{20,16},{24,... | collective-permute-start | bytes 1572872 | tf_op jit(solution)/shard_map/ppermute | solution.py:282
  (116 other events, 3504.7 us)
